TPU v7x, 256 devices: a whole 4x4x8 slice. The times are simulated.
256 devices in a mesh: group: 16 (over y, z_lo), expert: 16 (over x, z_hi, core).
Axes of the slice: x: 4, y: 4, z: 8 (z_hi: 2, z_lo: 4; z = z_hi * 4 + z_lo), core: 2. Of those that a mesh axis runs over, the one named last changes fastest.
Arguments:
- rows_in: bfloat16 [16384, 3584], P(('group', 'expert')), may hold values from -6 to 6
- expert_ids: int32 [16384, 2], P(('group', 'expert')), may hold values from 0 to 7, all different within a row; in each aligned block of 64 rows (0 to 63, 64 to 127, ...) at most 32 rows name the same one
- route_weight: float32 [16384, 2], P(('group', 'expert')), may hold values from 0.2 to 1
- gate_weight: bfloat16 [16, 3584, 512], P('expert'), may hold values from -0.09375 to 0.09375
- up_weight: bfloat16 [16, 3584, 512], P('expert'), may hold values from -0.09375 to 0.09375
- down_weight: bfloat16 [16, 512, 3584], P('expert'), may hold values from -0.1875 to 0.1875
- gate_b: bfloat16 [8, 3584, 64], P(None, 'group'), may hold values from -2 to 2
- gate_a: bfloat16 [16, 64, 512], P('expert', 'group'), may hold values from -0.15625 to 0.15625
- up_b: bfloat16 [8, 3584, 64], P(None, 'group'), may hold values from -2 to 2
- up_a: bfloat16 [16, 64, 512], P('expert', 'group'), may hold values from -0.15625 to 0.15625
- down_b: bfloat16 [16, 512, 64], P('expert', 'group'), may hold values from -2 to 2
- down_a: bfloat16 [8, 64, 3584], P(None, None, 'group'), may hold values from -0.25 to 0.25
Outputs:
- mixed: bfloat16 [16384, 3584], P(('group', 'expert'))
Inputs may be any that keep to these rules, and one draw needn't show every extreme that they name: `expert_ids`: each row names 2 different experts. Within each aligned block of 64 rows (the rows of one device) no expert is named by more than 32 rows, a bound that some block reaches.
All inputs are finite; a program needn't handle non-finite values.
Results may differ from a plain program's by a relative error of at most 0.0076.
Values may be sent and summed in bfloat16 or wider, within the bound.
A program may use at most 128 MiB of HBM per device.

v0:
```python
import jax
import jax.numpy as jnp
from jax import lax
from jax.sharding import PartitionSpec as P


def on_device(
    rows_in,
    expert_ids,
    route_weight,
    gate_weight,
    up_weight,
    down_weight,
    gate_b,
    gate_a,
    up_b,
    up_a,
    down_b,
    down_a,
):
    devices_expert = lax.axis_size("expert")
    own_index = lax.axis_index("expert")
    pair_index = own_index // 2
    expert_count = devices_expert // 2
    tok_rows, width = rows_in.shape
    top_count = expert_ids.shape[1]
    capacity = min(tok_rows, 2 * tok_rows * top_count // expert_count)
    own_gate_b = lax.dynamic_index_in_dim(gate_b, pair_index, 0, keepdims=False)
    own_up_b = lax.dynamic_index_in_dim(up_b, pair_index, 0, keepdims=False)
    own_down_a = lax.dynamic_index_in_dim(down_a, pair_index, 0, keepdims=False)
    full_gate_b, full_up_b, full_down_a, full_gate_a, full_up_a, full_down_b = (
        lax.all_gather(own_gate_b, "group", axis=0, tiled=True),
        lax.all_gather(own_up_b, "group", axis=0, tiled=True),
        lax.all_gather(own_down_a, "group", axis=1, tiled=True),
        lax.all_gather(gate_a[0], "group", axis=0, tiled=True),
        lax.all_gather(up_a[0], "group", axis=0, tiled=True),
        lax.all_gather(down_b[0], "group", axis=0, tiled=True),
    )
    named = expert_ids[:, :, None] == jnp.arange(expert_count, dtype=jnp.int32)[None, None, :]
    hits = jnp.sum(named.astype(jnp.int32), axis=1)
    place = jnp.cumsum(hits, axis=0) - hits
    slot_table = (hits.T[:, None, :] == 1) & (
        place.T[:, None, :] == jnp.arange(capacity, dtype=jnp.int32)[None, :, None]
    )
    slot_table = slot_table.astype(jnp.bfloat16)
    weight_of = jnp.sum(route_weight[:, :, None] * named.astype(jnp.float32), axis=1)
    buffer = jnp.einsum(
        "ecr,rd->ecd", slot_table, rows_in, preferred_element_type=jnp.float32
    ).astype(jnp.bfloat16)
    outgoing = jnp.repeat(buffer, 2, axis=0)
    received = lax.all_to_all(outgoing, "expert", split_axis=0, concat_axis=0, tiled=True)
    merged_gate = (
        gate_weight[0] + jnp.dot(full_gate_b, full_gate_a, preferred_element_type=jnp.float32)
    ).astype(jnp.bfloat16)
    merged_up = (
        up_weight[0] + jnp.dot(full_up_b, full_up_a, preferred_element_type=jnp.float32)
    ).astype(jnp.bfloat16)
    merged_down = (
        down_weight[0] + jnp.dot(full_down_b, full_down_a, preferred_element_type=jnp.float32)
    ).astype(jnp.bfloat16)
    flat_rows = received.reshape(devices_expert * capacity, width)
    gate_part = jnp.dot(flat_rows, merged_gate, preferred_element_type=jnp.float32)
    up_part = jnp.dot(flat_rows, merged_up, preferred_element_type=jnp.float32)
    hidden_part = (jax.nn.silu(gate_part) * up_part).astype(jnp.bfloat16)
    partial_value = jnp.dot(hidden_part, merged_down, preferred_element_type=jnp.float32)
    returned = lax.all_to_all(
        partial_value.reshape(devices_expert, capacity, width),
        "expert",
        split_axis=0,
        concat_axis=0,
        tiled=True,
    )
    expert_out = returned.reshape(expert_count, 2, capacity, width).sum(axis=1).astype(jnp.bfloat16)
    placed = jnp.einsum("ecr,ecd->erd", slot_table, expert_out, preferred_element_type=jnp.float32)
    mixed = jnp.sum(weight_of.T[:, :, None] * placed, axis=0)
    return mixed.astype(jnp.bfloat16)


def solution(mesh):
    return jax.shard_map(
        on_device,
        mesh=mesh,
        in_specs=(
            P(("group", "expert"), None),
            P(("group", "expert"), None),
            P(("group", "expert"), None),
            P("expert", None, None),
            P("expert", None, None),
            P("expert", None, None),
            P(None, "group", None),
            P("expert", "group", None),
            P(None, "group", None),
            P("expert", "group", None),
            P("expert", "group", None),
            P(None, None, "group"),
        ),
        out_specs=P(("group", "expert"), None),
        check_vma=False,
    )
```

profile of v0, /device:TPU:1, one launch (start us, length us, event | category | flops | bytes accessed | tf_op | source)
XLA Modules:
  0.0 602.8 jit_solution(12951687436399113708)
XLA Ops:
  0.0 0.0 copy-start
  0.0 0.7 convert_reduce_fusion
  0.7 0.1 copy.39
  0.8 0.1 reduce_window_sum.11
  0.9 0.1 copy.41
  1.0 0.0 copy-done
  1.0 0.6 convolution_convert_fusion
  1.7 2.2 broadcast_in_dim.2
  3.9 12.4 %all-to-all-start = ((bf16[16,32,3584]{2,1,0:T(8,128)(2,1)}), bf16[16,32,3584]{2,1,0:T(8,128)(2,1)}, u32[]{:S(2)}, u32[]{:S(2)}) async-start(bf16[16,32,3584]{2,1,0:T(8,128)(2,1)} %bitcast.64), calls=%async_computation | async-start | bytes 7340032 | tf_op jit(solution)/shard_map/all_to_all | solution.py:51
  16.3 0.0 copy-start.3
  16.3 0.8 constant_dynamic-slice_fusion.2
  17.1 0.1 copy.53
  17.2 130.3 %all-gather = bf16[1,3584,64]{2,0,1:T(2,128)(2,1)S(1)} all-gather(bf16[1,224,64]{2,0,1:T(2,128)(2,1)S(1)} %copy.53), channel_id=2, replica_groups=mesh['group'=16,'expert'=16] {'group'}, dimensions={1}, use_global_device_ids=true | all-gather | bytes 487424 | tf_op jit(solution)/shard_map/all_gather | solution.py:32
  147.5 0.0 copy-start.4
  147.5 2.0 copy.43
  149.5 0.0 copy-done.3
  149.6 0.8 constant_dynamic-slice_fusion.1
  150.3 0.1 copy.54
  150.4 52.1 %all-gather.2 = bf16[1,3584,64]{2,0,1:T(2,128)(2,1)S(1)} all-gather(bf16[1,224,64]{2,0,1:T(2,128)(2,1)S(1)} %copy.54), channel_id=4, replica_groups=mesh['group'=16,'expert'=16] {'group'}, dimensions={1}, use_global_device_ids=true | all-gather | bytes 487424 | tf_op jit(solution)/shard_map/all_gather | solution.py:33
  202.6 2.0 copy.46
  204.6 0.0 copy-done.4
  204.7 0.8 constant_dynamic-slice_fusion
  205.4 0.1 copy.55
  205.5 52.3 %all-gather.4 = bf16[1,64,3584]{1,0,2:T(2,128)(2,1)S(1)} all-gather(bf16[1,64,224]{1,0,2:T(2,128)(2,1)S(1)} %copy.55), channel_id=6, replica_groups=mesh['group'=16,'expert'=16] {'group'}, dimensions={2}, use_global_device_ids=true | all-gather | bytes 487424 | tf_op jit(solution)/shard_map/all_gather | solution.py:34
  257.8 3.1 copy.50
  260.9 0.0 copy-start.2
  260.9 6.0 copy.48
  266.9 31.0 %all-gather.1 = bf16[1,64,512]{2,0,1:T(2,128)(2,1)S(1)} all-gather(bf16[1,4,512]{2,0,1:T(2,128)(2,1)S(1)} %copy.44), channel_id=3, replica_groups=mesh['group'=16,'expert'=16] {'group'}, dimensions={1}, use_global_device_ids=true | all-gather | bytes 69632 | tf_op jit(solution)/shard_map/all_gather | solution.py:35
  297.9 32.7 %all-gather.3 = bf16[1,64,512]{2,0,1:T(2,128)(2,1)S(1)} all-gather(bf16[1,4,512]{2,0,1:T(2,128)(2,1)S(1)} %copy.47), channel_id=5, replica_groups=mesh['group'=16,'expert'=16] {'group'}, dimensions={1}, use_global_device_ids=true | all-gather | bytes 69632 | tf_op jit(solution)/shard_map/all_gather | solution.py:36
  330.6 0.0 copy-done.2
  330.6 31.5 %all-gather.5 = bf16[1,512,64]{2,1,0:T(8,128)(2,1)S(1)} all-gather(bf16[1,32,64]{2,1,0:T(8,128)(2,1)S(1)} %copy-done.2), channel_id=7, replica_groups=mesh['group'=16,'expert'=16] {'group'}, dimensions={1}, use_global_device_ids=true | all-gather | bytes 69632 | tf_op jit(solution)/shard_map/all_gather | solution.py:37
  362.1 0.0 all-to-all-done
  362.1 7.2 %fusion.5 = f32[512,512]{1,0:T(8,128)} fusion(bf16[512,3584]{1,0:T(8,128)(2,1)} %bitcast.5, bf16[1,3584,512]{2,1,0:T(8,128)(2,1)} %param.15, bf16[1,3584,64]{1,2,0:T(8,128)(2,1)S(1)} %copy.43, bf16[1,64,512]{2,0,1:T(2,128)(2,1)S(1)} %all-gather.1), kind=kOutput, calls=%fused_computation.11 | convolution fusion | flops 2119434240 | bytes 8912896 | tf_op jit(solution)/shard_map/dot_general | solution.py:62
  369.2 0.0 copy-start.1
  369.2 6.5 %fusion.8 = bf16[512,512]{1,0:T(8,128)(2,1)S(1)} fusion(bf16[512,3584]{1,0:T(8,128)(2,1)} %bitcast.5, bf16[1,3584,512]{2,1,0:T(8,128)(2,1)} %param.16, f32[512,512]{1,0:T(8,128)} %fusion.5, bf16[1,3584,64]{1,2,0:T(8,128)(2,1)S(1)} %copy.46, bf16[1,64,512]{2,0,1:T(2,128)(2,1)S(1)} %all-gather.3), kind=kOutput, calls=%fused_computation.14 | convolution fusion | flops 2121007104 | bytes 9437184 | tf_op jit(solution)/shard_map/dot_general | solution.py:63
  375.8 0.0 copy-done.1
  375.8 8.1 %fusion.4 = f32[512,3584]{1,0:T(8,128)} fusion(bf16[512,512]{1,0:T(8,128)(2,1)S(1)} %fusion.8, bf16[1,512,3584]{1,2,0:T(8,128)(2,1)} %copy.48, bf16[1,64,3584]{2,1,0:T(8,128)(2,1)S(1)} %copy-done.1, bf16[1,512,64]{2,1,0:T(8,128)(2,1)S(1)} %all-gather.5), kind=kOutput, calls=%fused_computation.10 | convolution fusion | flops 2119434240 | bytes 12058624 | tf_op jit(solution)/shard_map/dot_general | solution.py:65
  383.8 0.0 copy-start.5
  383.8 0.0 copy-start.6
  383.8 49.5 %all-to-all-start.1 = ((f32[16,32,3584]{2,1,0:T(8,128)}), f32[16,32,3584]{2,1,0:T(8,128)}, u32[]{:S(2)}, u32[]{:S(2)}) async-start(f32[16,32,3584]{2,1,0:T(8,128)} %bitcast.65), calls=%async_computation.1 | async-start | bytes 14680064 | tf_op jit(solution)/shard_map/all_to_all | solution.py:66
  433.3 0.0 copy-done.5
  433.4 0.0 copy-done.6
  433.4 163.3 %all-to-all-done.1 = f32[16,32,3584]{2,1,0:T(8,128)} async-done(((f32[16,32,3584]{2,1,0:T(8,128)}), f32[16,32,3584]{2,1,0:T(8,128)}, u32[]{:S(2)}, u32[]{:S(2)}) %all-to-all-start.1) | async-done | bytes 7340064 | tf_op jit(solution)/shard_map/all_to_all | solution.py:66
  596.7 4.1 bitcast_reduce_fusion
  600.8 1.9 multiply_reduce_fusion
  (5 shorter events, 0.0 us)
Async XLA Ops:
  0.0 1.0 copy-start
  3.9 358.2 %all-to-all-start = ((bf16[16,32,3584]{2,1,0:T(8,128)(2,1)}), bf16[16,32,3584]{2,1,0:T(8,128)(2,1)}, u32[]{:S(2)}, u32[]{:S(2)}) async-start(bf16[16,32,3584]{2,1,0:T(8,128)(2,1)} %bitcast.64), calls=%async_computation | async-start | bytes 7340032 | tf_op jit(solution)/shard_map/all_to_all | solution.py:51
  16.3 133.2 %copy-start.3 = (bf16[1,4,512]{2,1,0:T(4,128)(2,1)S(1)}, bf16[1,4,512]{2,1,0:T(4,128)(2,1)}, u32[]{:S(2)}) copy-start(bf16[1,4,512]{2,1,0:T(4,128)(2,1)} %param.19) | copy-start | bytes 12292
  147.5 57.1 %copy-start.4 = (bf16[1,4,512]{2,1,0:T(4,128)(2,1)S(1)}, bf16[1,4,512]{2,1,0:T(4,128)(2,1)}, u32[]{:S(2)}) copy-start(bf16[1,4,512]{2,1,0:T(4,128)(2,1)} %param.21) | copy-start | bytes 12292
  260.9 69.6 %copy-start.2 = (bf16[1,32,64]{2,1,0:T(8,128)(2,1)S(1)}, bf16[1,32,64]{2,1,0:T(8,128)(2,1)}, u32[]{:S(2)}) copy-start(bf16[1,32,64]{2,1,0:T(8,128)(2,1)} %param.22) | copy-start | bytes 12292
  369.2 6.5 %copy-start.1 = (bf16[1,64,3584]{2,1,0:T(8,128)(2,1)S(1)}, bf16[1,64,3584]{2,1,0:T(8,128)(2,1)}, u32[]{:S(2)}) copy-start(bf16[1,64,3584]{2,1,0:T(8,128)(2,1)} %copy.50) | copy-start | bytes 1376260
  383.8 49.5 %copy-start.5 = (s32[64,2]{0,1:T(2,128)S(1)}, s32[64,2]{0,1:T(2,128)}, u32[]{:S(2)}) copy-start(s32[64,2]{0,1:T(2,128)} %param.13) | copy-start | bytes 1540
  383.8 49.5 %copy-start.6 = (f32[64,2]{0,1:T(2,128)S(1)}, f32[64,2]{0,1:T(2,128)}, u32[]{:S(2)}) copy-start(f32[64,2]{0,1:T(2,128)} %param.14) | copy-start | bytes 1540
  383.8 212.9 %all-to-all-start.1 = ((f32[16,32,3584]{2,1,0:T(8,128)}), f32[16,32,3584]{2,1,0:T(8,128)}, u32[]{:S(2)}, u32[]{:S(2)}) async-start(f32[16,32,3584]{2,1,0:T(8,128)} %bitcast.65), calls=%async_computation.1 | async-start | bytes 14680064 | tf_op jit(solution)/shard_map/all_to_all | solution.py:66
where the time goes:
time: 603 us
  blocking collectives  330 us (55%)
  waiting for transfers between devices  163 us (27%)
  starting transfers between devices  61.9 us (10%)
  matrix products  24.3 us (4%)
  local copies, waits for them, and re-layouts  18.2 us (3%)
    all_to_all x1, waiting for transfers between devices, on_device(): lax.all_to_all(partial_value.reshape(devices_expert, capacity, width), 'e...  163 us
    all_gather x1, blocking collectives, on_device(): lax.all_gather(own_gate_b, 'group', axis=0, tiled=True)  130 us
    all_gather x1, blocking collectives, on_device(): lax.all_gather(own_down_a, 'group', axis=1, tiled=True)  52.3 us
    all_gather x1, blocking collectives, on_device(): lax.all_gather(own_up_b, 'group', axis=0, tiled=True)  52.1 us
    all_to_all x1, starting transfers between devices, on_device(): lax.all_to_all(partial_value.reshape(devices_expert, capacity, width), 'e...  49.5 us
    all_gather x1, blocking collectives, on_device(): lax.all_gather(up_a[0], 'group', axis=0, tiled=True)  32.7 us
    all_gather x1, blocking collectives, on_device(): lax.all_gather(down_b[0], 'group', axis=0, tiled=True)  31.5 us
    all_gather x1, blocking collectives, on_device(): lax.all_gather(gate_a[0], 'group', axis=0, tiled=True)  31 us
  transfers between devices with their start and end apart: 2, of which 1 were waited for; matrix products, arithmetic and copies ran while one was open for 3% of the time, Pallas kernels for 0%

commit v1 on v0

v1 whole, which is shorter than its diff:
```python
import jax
import jax.numpy as jnp
from jax import lax
from jax.experimental import pallas as pl
from jax.experimental.pallas import tpu as pltpu
from jax.sharding import PartitionSpec as P

MESH = pl.DeviceIdType.MESH
BF = jnp.bfloat16
F32 = jnp.float32

D = 3584
HID = 512
ROWS = 64
CAP = 32
RANK = 64
KC = 512
NK = D // KC
HALF = D // 2
JC = 256
NJ = HALF // JC
SHARD = 224
PART = SHARD // 2


def iota(shape, dim):
    return lax.broadcasted_iota(jnp.int32, shape, dim)


def onehot(mask):
    return jnp.where(mask, 1.0, 0.0).astype(BF)


def dot(a, b):
    return jnp.dot(a, b, preferred_element_type=F32)


def dot_nt(a, b):
    return lax.dot_general(a, b, (((1,), (1,)), ((), ())), preferred_element_type=F32)


def split(v):
    high = v.astype(BF)
    return high, (v - high.astype(F32)).astype(BF)


def kernel(
    rows, ids, wts, gate_w, up_w, down_w, gate_b, gate_a, up_b, up_a, down_b, down_a,
    out,
    rw, meta, tab, wtab, sel, got, w, dw, acc, low, hid, back, back_got,
    pack_g, pack_u, pack_d, fac, gub, daf, dbf, a2,
    zs, zr, own, fin, fin_got,
    s_load, s_w, s_dw, s_meta, s_zrow, r_zrow, r_meta,
    s_x, r_x, s_fwd, r_fwd, s_dwx, r_dwx, s_fac, r_facz, r_facy, r_facd,
    s_hid, r_hid, s_ret, r_ret, s_zret, r_zret, s_fin, r_fin,
):
    g = lax.axis_index("group")
    e = lax.axis_index("expert")
    y, zl = g // 4, g % 4
    x, zh, c = e // 4, (e // 2) % 2, e % 2
    pair = e // 2

    def dev(y_, zl_, x_, zh_, c_):
        return (y_ * 4 + zl_, (x_ * 2 + zh_) * 2 + c_)

    sibling = dev(y, zl, x, zh, 1 - c)
    mirror = dev(y, 3 - zl, x, 1 - zh, c)
    x_up = [dev(y, zl, (x + d) % 4, zh, c) for d in (1, 2, 3)]
    x_down = [dev(y, zl, (x + 4 - d) % 4, zh, c) for d in (1, 2, 3)]
    z_peers = [dev(y, (zl + d) % 4, x, zh, c) for d in (1, 2, 3)]
    y_peers = [dev((y + d) % 4, zl, x, zh, c) for d in (1, 2, 3)]
    far = jnp.where((zl == 1) | (zl == 2), 1, 0)
    first, second = far, 1 - far

    def remote(src, dst, ssem, rsem, target):
        return pltpu.make_async_remote_copy(
            src_ref=src, dst_ref=dst, send_sem=ssem, recv_sem=rsem,
            device_id=target, device_id_type=MESH)

    def wait_bytes(ref, sem):
        pltpu.make_async_copy(ref, ref, sem).wait()

    loads = [
        pltpu.make_async_copy(gate_b.at[pair], pack_g, s_load.at[0]),
        pltpu.make_async_copy(up_b.at[pair], pack_u, s_load.at[1]),
        pltpu.make_async_copy(down_a.at[pair], pack_d, s_load.at[2]),
    ]
    for copy in loads:
        copy.start()

    def row_load(k):
        return pltpu.make_async_copy(
            rows.at[:, pl.ds(pl.multiple_of(k * KC, KC), KC)], rw.at[0, k], s_load.at[3 + k])

    def w_load(k, part):
        src = (gate_w, up_w)[part]
        return pltpu.make_async_copy(
            src.at[0, pl.ds(pl.multiple_of(k * KC, KC), KC), :],
            w.at[k, :, pl.ds(part * HID, HID)], s_w.at[k, part])

    def dw_cols(core, j):
        return down_w.at[0, :, pl.ds(pl.multiple_of(core * HALF + j * JC, JC), JC)]

    def dw_load(j):
        return pltpu.make_async_copy(dw_cols(c, j), dw.at[c, j], s_dw.at[j])

    def dw_send(j):
        return remote(dw_cols(1 - c, j), dw.at[c, j], s_dwx.at[j], r_dwx.at[j], sibling)

    @pl.loop(0, NK)
    def _(k):
        row_load(k).start()

    @pl.loop(0, NK)
    def _(k):
        w_load(k, 0).start()
        w_load(k, 1).start()

    barrier = pltpu.get_barrier_semaphore()
    peers = [sibling, mirror] + x_up + z_peers + y_peers
    for peer in peers:
        pl.semaphore_signal(barrier, inc=1, device_id=peer, device_id_type=MESH)

    lane = iota((ROWS, 128), 1)
    idf = ids[...].astype(F32)
    wt = wts[...]
    meta[0, c] = jnp.where(
        lane == 0, idf[:, 0:1],
        jnp.where(lane == 1, idf[:, 1:2], jnp.where(lane == 2, wt[:, 0:1], wt[:, 1:2])))

    pl.semaphore_wait(barrier, len(peers))

    meta_mirror = remote(meta.at[0, c], meta.at[1, c], s_meta.at[0], r_meta.at[0], mirror)
    meta_sibling = remote(meta.at[0, c], meta.at[0, c], s_meta.at[1], r_meta.at[1], sibling)
    meta_second = remote(meta.at[1, c], meta.at[1, c], s_meta.at[2], r_meta.at[2], sibling)
    meta_mirror.start()
    meta_sibling.start()

    def zrow(k):
        return remote(
            rows.at[:, pl.ds(pl.multiple_of(k * KC, KC), KC)], rw.at[1, k],
            s_zrow.at[k], r_zrow.at[k], mirror)

    @pl.when(far == 0)
    def _():
        @pl.loop(0, NK)
        def _(k):
            zrow(k).start()

    for copy in loads:
        copy.wait()
    half = pl.ds(pl.multiple_of(c * PART, 16), PART)
    left64 = onehot(iota((64, 128), 0) == iota((64, 128), 1))
    right64 = onehot(iota((64, 128), 0) + 64 == iota((64, 128), 1))
    packed = dot(pack_g[half, :], left64) + dot(pack_u[half, :], right64)
    mine = fac.at[y, zl, c]
    mine[:, 0:128] = packed.astype(BF)
    pick = onehot(iota((PART, SHARD), 1) == iota((PART, SHARD), 0) + c * PART)
    turned = dot_nt(pick, pack_d[...]).astype(BF)
    placed = dot(onehot(iota((PART, 32), 0) == iota((PART, 32), 1)), down_b[0]).astype(BF)
    row = iota((PART, 4), 0) - 32
    fits = (row >= 0) & (row < 64)
    which = (row + 32) % 8
    col = iota((PART, 4), 1)
    spread = (dot(onehot(fits & (which == col)), gate_a[0])
              + dot(onehot(fits & (which == col + 4)), up_a[0]))
    block = (iota((PART, HID), 0) - 32) // 8
    spread = jnp.where(block == iota((PART, HID), 1) // 64, spread, 0.0).astype(BF)
    fold = onehot(iota((HID, 128), 0) % 64 + 64 == iota((HID, 128), 1))
    packed = dot(turned, left64) + dot(placed, right64) + dot(spread, fold)
    mine[:, 128:256] = packed.astype(BF)

    for d in range(3):
        remote(fac.at[y, zl, c], fac.at[y, zl, c], s_fac.at[0], r_facz, z_peers[d]).start()

    @pl.when(far == 1)
    def _():
        @pl.loop(0, NK)
        def _(k):
            zrow(k).start()

    @pl.loop(0, NJ)
    def _(j):
        dw_load(j).start()
        dw_send(j).start()

    def tables(m):
        lane = iota((ROWS, 128), 1)
        expert = (((x + lane // 32) % 4) * 2 + zh).astype(F32)
        hit0, hit1 = m[:, 0:1] == expert, m[:, 1:2] == expert
        hit = jnp.where(hit0, 1.0, 0.0) + jnp.where(hit1, 1.0, 0.0)
        before = onehot(iota((ROWS, ROWS), 1) < iota((ROWS, ROWS), 0))
        place = dot(before, hit.astype(BF))
        table = jnp.where(place == (lane % 32).astype(F32), hit, 0.0)
        weight = jnp.where(hit0, m[:, 2:3], 0.0) + jnp.where(hit1, m[:, 3:4], 0.0)
        return table, table * weight

    def make_select(om):
        table, weight = tables(meta[om, c])
        tab[om] = table.T.astype(BF)
        high, rest = split(weight)
        wtab[om, c, 0:ROWS, :] = high
        wtab[om, c, ROWS:2 * ROWS, :] = rest

    def make_weights(om, cs):
        _, weight = tables(meta[om, cs])
        high, rest = split(weight)
        wtab[om, cs, 0:ROWS, :] = high
        wtab[om, cs, ROWS:2 * ROWS, :] = rest

    def dispatch(om, k):
        @pl.when(om == 0)
        def _():
            row_load(k).wait()

        @pl.when(om == 1)
        def _():
            zrow(k).wait_recv()

        value = dot(tab[om], rw[om, k]).astype(BF)
        got[om, k, 0, c] = value[0:CAP]
        sel[om, k] = value[CAP:].reshape(3, CAP, KC)
        for d in range(3):
            remote(sel.at[om, k, d], got.at[om, k, d + 1, c], s_x, r_x.at[om, k], x_up[d]).start()

    def forward(om, k):
        return remote(got.at[om, k, :, c], got.at[om, k, :, c],
                      s_fwd.at[om, k], r_fwd.at[om, k], sibling)

    def arrive(om, k):
        wait_bytes(sel.at[om, k], r_x.at[om, k])
        forward(om, k).start()

    def gate_up(om, k):
        forward(om, k).wait_recv()
        value = got[om, k].reshape(8 * CAP, KC)
        for n in range(4):
            cols = pl.ds(n * 256, 256)
            part = dot(value, w[k, :, cols])

            @pl.when(k == 0)
            def _():
                acc[om, :, cols] = part

            @pl.when(k > 0)
            def _():
                acc[om, :, cols] += part

    make_select(0)

    @pl.when(far == 1)
    def _():
        meta_mirror.wait_recv()
        meta_second.start()
        make_select(1)

    @pl.loop(0, 3)
    def _(k):
        dispatch(first, k)

    wait_bytes(fac.at[0, pl.ds(0, 3), 0], r_facz)
    for d in range(3):
        remote(fac.at[y, :, c], fac.at[y, :, c], s_fac.at[1], r_facy, y_peers[d]).start()

    @pl.loop(3, NK)
    def _(k):
        dispatch(first, k)

    @pl.when(far == 0)
    def _():
        meta_mirror.wait_recv()
        meta_second.start()
        make_select(1)

    @pl.loop(0, NK + 1)
    def _(k):
        @pl.when(k < NK)
        def _():
            dispatch(second, k)
            arrive(first, k)
            w_load(k, 0).wait()
            w_load(k, 1).wait()

        @pl.when(k > 0)
        def _():
            gate_up(first, k - 1)

    wait_bytes(fac.at[pl.ds(0, 3), :, 0], r_facy)
    fac_forward = remote(fac.at[:, :, c], fac.at[:, :, c], s_fac.at[2], r_facd, sibling)
    fac_forward.start()
    meta_sibling.wait_recv()
    meta_second.wait_recv()
    make_weights(0, 1 - c)
    make_weights(1, 1 - c)
    fac_forward.wait_recv()

    left = iota((896, 128), 1) < 64
    for yy in range(4):
        gub[pl.ds(yy * 896, 896), :] = fac[yy, :, :, :, 0:128].reshape(896, 128)
        part = fac[yy, :, :, :, 128:256].reshape(896, 128).astype(F32)
        part = jnp.where(left, part, 0.0)
        daf[pl.ds(yy * 896, 896), :] = (part + pltpu.roll(part, 64, 1)).astype(BF)
        for core in range(2):
            part = fac[yy, :, core, 0:32, 128:256].reshape(128, 128)
            dbf[core, pl.ds(yy * 128, 128), :] = jnp.where(
                iota((128, 128), 1) < 64, jnp.zeros_like(part), part)
    small = fac[:, :, c, 32:96, 128:256].reshape(1024, 128)
    unfold = onehot((iota((128, HID), 1) % 64 + 64) == iota((128, HID), 0))
    wide = dot(small, unfold)
    block = (iota((1024, HID), 0) % 64) // 8
    wide = jnp.where(block == iota((1024, HID), 1) // 64, wide, 0.0).astype(BF)
    r = iota((128, 1024), 0)
    s = iota((128, 1024), 1)
    take = onehot((s // 64 == (r % 64) // 4) & (s % 8 == r % 4 + 4 * (r // 64)))
    right = dot(take, wide).astype(BF)
    upper = iota((128, HID), 0) < 64
    for n in range(2):
        rs = pl.ds(n * 128, 128)
        a2[rs, 0:HID] = jnp.where(upper, right, jnp.zeros_like(right))
        a2[rs, HID:2 * HID] = jnp.where(upper, jnp.zeros_like(right), right)

    def hidden(om):
        low[...] = jnp.zeros_like(low)

        @pl.loop(0, NK)
        def _(k):
            low[...] += dot(got[om, k].reshape(8 * CAP, KC),
                            gub[pl.ds(pl.multiple_of(k * KC, KC), KC), :])

        high, rest = split(low[...])
        both = jnp.concatenate([high, rest], axis=1)
        for n in range(2):
            cols, ups = pl.ds(n * 256, 256), pl.ds(HID + n * 256, 256)
            gate = acc[om, :, cols] + dot(both, a2[:, cols])
            up = acc[om, :, ups] + dot(both, a2[:, ups])
            hid[om, c, :, cols] = (gate / (1.0 + jnp.exp(-gate)) * up).astype(BF)
        hid_send(om).start()

    def hid_send(om):
        return remote(hid.at[om, c], hid.at[om, c], s_hid.at[om], r_hid.at[om], sibling)

    def low_down(om):
        hid_send(om).wait_recv()
        value = dot(hid[om, 0], dbf[0]) + dot(hid[om, 1], dbf[1])
        high, rest = split(value)
        low2 = high.astype(F32) + pltpu.roll(rest.astype(F32), 64, 1)
        return low2.astype(BF)

    def down(om, j, low2):
        da = daf[pl.ds(pl.multiple_of(c * HALF + j * JC, JC), JC), :]
        value = dot(hid[om, 0], dw[0, j]) + dot(hid[om, 1], dw[1, j]) + dot_nt(low2, da)
        value = value.astype(BF).reshape(4, 2, CAP, JC)
        back_got[om, j, 0] = value[0]
        back[om, j] = value[1:]
        for d in range(3):
            remote(back.at[om, j, d], back_got.at[om, j, d + 1],
                   s_ret, r_ret.at[om, j], x_down[d]).start()

    def zret(j):
        return remote(zs.at[j], zr.at[j], s_zret.at[j], r_zret.at[j], mirror)

    def combine(om, j):
        wait_bytes(back.at[om, j], r_ret.at[om, j])
        for cs in range(2):
            value = dot(wtab[om, cs], back_got[om, j, :, cs].reshape(4 * CAP, JC))
            value = value[0:ROWS] + value[ROWS:]

            @pl.when(om == 0)
            def _():
                own[j, cs] = value

            @pl.when(om == 1)
            def _():
                zs[j, cs] = value.astype(BF)

        @pl.when(om == 1)
        def _():
            zret(j).start()

    def fin_send(j):
        return remote(fin.at[j], fin_got.at[j], s_fin.at[j], r_fin.at[j], sibling)

    def finish(j):
        zret(j).wait_recv()
        fin[j] = (own[j, 1 - c] + zr[j, 1 - c].astype(F32)).astype(BF)
        fin_send(j).start()
        cols = pl.ds(pl.multiple_of(c * HALF + j * JC, JC), JC)
        out[:, cols] = (own[j, c] + zr[j, c].astype(F32)).astype(BF)

    hidden(first)

    @pl.loop(0, NJ)
    def _(j):
        dw_load(j).wait()
        dw_send(j).wait_recv()

    low_first = low_down(first)

    @pl.loop(0, NK + 1)
    def _(k):
        @pl.when(k < NK)
        def _():
            arrive(second, k)
            down(first, k, low_first)

        @pl.when(k > 0)
        def _():
            gate_up(second, k - 1)

    hidden(second)

    @pl.loop(0, 3)
    def _(j):
        combine(first, j)

    low_second = low_down(second)

    @pl.loop(0, NJ)
    def _(j):
        down(second, j, low_second)

        @pl.when(j + 3 < NJ)
        def _():
            combine(first, j + 3)

    @pl.loop(0, NJ)
    def _(j):
        combine(second, j)

    @pl.loop(0, NJ)
    def _(j):
        finish(j)

    @pl.loop(0, NJ)
    def _(j):
        fin_send(j).wait_recv()
        cols = pl.ds(pl.multiple_of((1 - c) * HALF + j * JC, JC), JC)
        out[:, cols] = fin_got[j]

    meta_mirror.wait_send()
    meta_sibling.wait_send()
    meta_second.wait_send()
    wait_bytes(sel, s_x)
    wait_bytes(back, s_ret)
    wait_bytes(fac.at[0, pl.ds(0, 3), 0], s_fac.at[0])
    wait_bytes(fac.at[pl.ds(0, 3), :, 0], s_fac.at[1])
    fac_forward.wait_send()
    for om in range(2):
        hid_send(om).wait_send()

        @pl.loop(0, NK)
        def _(k):
            forward(om, k).wait_send()

    @pl.loop(0, NJ)
    def _(j):
        zrow(j).wait_send()
        dw_send(j).wait_send()
        zret(j).wait_send()
        fin_send(j).wait_send()


def on_device(*args):
    vmem = pl.BlockSpec(memory_space=pltpu.VMEM)
    hbm = pl.BlockSpec(memory_space=pl.ANY)
    dma = pltpu.SemaphoreType.DMA
    scratch = [
        pltpu.VMEM((2, NK, ROWS, KC), BF),
        pltpu.VMEM((2, 2, ROWS, 128), F32),
        pltpu.VMEM((2, 128, ROWS), BF),
        pltpu.VMEM((2, 2, 2 * ROWS, 128), BF),
        pltpu.VMEM((2, NK, 3, CAP, KC), BF),
        pltpu.VMEM((2, NK, 4, 2, CAP, KC), BF),
        pltpu.VMEM((NK, KC, 2 * HID), BF),
        pltpu.VMEM((2, NJ, HID, JC), BF),
        pltpu.VMEM((2, 8 * CAP, 2 * HID), F32),
        pltpu.VMEM((8 * CAP, 128), F32),
        pltpu.VMEM((2, 2, 8 * CAP, HID), BF),
        pltpu.VMEM((2, NJ, 3, 2, CAP, JC), BF),
        pltpu.VMEM((2, NJ, 4, 2, CAP, JC), BF),
        pltpu.VMEM((SHARD, RANK), BF),
        pltpu.VMEM((SHARD, RANK), BF),
        pltpu.VMEM((RANK, SHARD), BF),
        pltpu.VMEM((4, 4, 2, PART, 256), BF),
        pltpu.VMEM((D, 128), BF),
        pltpu.VMEM((D, 128), BF),
        pltpu.VMEM((2, HID, 128), BF),
        pltpu.VMEM((256, 2 * HID), BF),
        pltpu.VMEM((NJ, 2, ROWS, JC), BF),
        pltpu.VMEM((NJ, 2, ROWS, JC), BF),
        pltpu.VMEM((NJ, 2, ROWS, JC), F32),
        pltpu.VMEM((NJ, ROWS, JC), BF),
        pltpu.VMEM((NJ, ROWS, JC), BF),
        dma((3 + NK,)),
        dma((NK, 2)),
        dma((NJ,)),
        dma((3,)),
        dma((NK,)),
        dma((NK,)),
        dma((3,)),
        dma,
        dma((2, NK)),
        dma((2, NK)),
        dma((2, NK)),
        dma((NJ,)),
        dma((NJ,)),
        dma((3,)),
        dma,
        dma,
        dma,
        dma((2,)),
        dma((2,)),
        dma,
        dma((2, NJ)),
        dma((NJ,)),
        dma((NJ,)),
        dma((NJ,)),
        dma((NJ,)),
    ]
    return pl.pallas_call(
        kernel,
        out_shape=jax.ShapeDtypeStruct((ROWS, D), BF),
        in_specs=[hbm, vmem, vmem, hbm, hbm, hbm, hbm, vmem, hbm, vmem, vmem, hbm],
        out_specs=vmem,
        scratch_shapes=scratch,
        compiler_params=pltpu.CompilerParams(
            collective_id=0, has_side_effects=True, vmem_limit_bytes=48 << 20),
        cost_estimate=pl.CostEstimate(
            flops=8 << 30, bytes_accessed=13 << 20, transcendentals=1 << 18),
        name="expert_layer",
    )(*args)


def solution(mesh):
    return jax.shard_map(
        on_device,
        mesh=mesh,
        in_specs=(
            P(("group", "expert"), None),
            P(("group", "expert"), None),
            P(("group", "expert"), None),
            P("expert", None, None),
            P("expert", None, None),
            P("expert", None, None),
            P(None, "group", None),
            P("expert", "group", None),
            P(None, "group", None),
            P("expert", "group", None),
            P("expert", "group", None),
            P(None, None, "group"),
        ),
        out_specs=P(("group", "expert"), None),
        check_vma=False,
    )
```

time: 603 us -> 94.2 us (0.16)
  blocking collectives: 330 us -> 0 us
  waiting for transfers between devices: 163 us -> 0 us
  Pallas kernels: 0 us -> 83.1 us
  starting transfers between devices: 61.9 us -> 0 us
  matrix products: 24.3 us -> 0 us
  local copies, waits for them, and re-layouts: 18.2 us -> 10.8 us
    all_gather x6 -> x0, blocking collectives: 330 us -> none  [the longest x1 130 us: on_device(): lax.all_gather(own_gate_b, 'group', axis=0, tiled=True)]
    all_to_all x2 -> x0, waiting for transfers between devices: 163 us -> none  [the longest x1 163 us: on_device(): lax.all_to_all(partial_value.reshape(devices_expert, capacity, width), 'e...]
    pallas_call x0 -> x1, Pallas kernels: none -> 83.1 us  [on_device(): pl.pallas_call(kernel, out_shape=jax.ShapeDtypeStruct((ROWS, D), BF), in_...]
    all_to_all x2 -> x0, starting transfers between devices: 61.9 us -> none  [the longest x1 49.5 us: on_device(): lax.all_to_all(partial_value.reshape(devices_expert, capacity, width), 'e...]
    dot_general x5 -> x0, matrix products: 24.3 us -> none  [the longest x1 8.06 us: on_device(): jnp.dot(hidden_part, merged_down, preferred_element_type=jnp.float32)]
    all_gather x3 -> x0, local copies, waits for them, and re-layouts: 7.14 us -> none  [the longest x1 3.08 us: on_device(): lax.all_gather(own_down_a, 'group', axis=1, tiled=True)]
  transfers between devices with their start and end apart: 2 -> 0, of which waited for: 1 -> 0; matrix products, arithmetic and copies ran while one was open for 3% -> 0% of each run, Pallas kernels for 0% -> 0%
where the time goes in v1:
time: 94.2 us; the launch traced here: 93.8 us
  Pallas kernels  83.1 us (88%)
  local copies, waits for them, and re-layouts  10.8 us (11%)
    pallas_call x1, Pallas kernels, on_device(): pl.pallas_call(kernel, out_shape=jax.ShapeDtypeStruct((ROWS, D), BF), in_...  83.1 us
    unnamed x17, local copies, waits for them, and re-layouts  10.8 us

profile of v1, /device:TPU:1, one launch (start us, length us, event | category | flops | bytes accessed | tf_op | source)
XLA Modules:
  0.0 93.8 jit_solution(14116577871238769798)
XLA Ops:
  0.0 0.8 copy.13.ids
  0.8 0.8 copy.14.wts
  1.5 1.2 %copy.15.gate_b = bf16[8,224,64]{2,1,0:T(8,128)(2,1)S(1)} copy(bf16[8,224,64]{1,2,0:T(8,128)(2,1)} %param.18) | data formatting | bytes 458752 | tf_op args[6]
  2.7 1.2 %copy.16.up_b = bf16[8,224,64]{2,1,0:T(8,128)(2,1)S(1)} copy(bf16[8,224,64]{1,2,0:T(8,128)(2,1)} %param.20) | data formatting | bytes 458752 | tf_op args[8]
  3.9 0.0 copy-start
  3.9 2.0 %copy-done = bf16[1,3584,512]{2,1,0:T(8,128)(2,1)S(1)} copy-done((bf16[1,3584,512]{2,1,0:T(8,128)(2,1)S(1)}, bf16[1,3584,512]{2,1,0:T(8,128)(2,1)}, u32[]{:S(2)}) %copy-start) | copy-done | bytes 3670040
  6.0 0.0 copy-start.1
  6.0 1.0 %copy-done.1 = bf16[64,3584]{1,0:T(8,128)(2,1)S(1)} copy-done((bf16[64,3584]{1,0:T(8,128)(2,1)S(1)}, bf16[64,3584]{1,0:T(8,128)(2,1)}, u32[]{:S(2)}) %copy-start.1) | copy-done | bytes 458776
  7.0 0.0 copy-start.2
  7.0 0.9 %copy-done.2 = bf16[8,64,224]{2,1,0:T(8,128)(2,1)S(1)} copy-done((bf16[8,64,224]{2,1,0:T(8,128)(2,1)S(1)}, bf16[8,64,224]{2,1,0:T(8,128)(2,1)}, u32[]{:S(2)}) %copy-start.2) | copy-done | bytes 229400
  7.9 0.0 copy-start.3
  7.9 0.7 copy-done.3
  8.6 0.0 copy-start.4
  8.6 0.7 copy-done.4
  9.3 0.0 copy-start.5
  9.3 0.7 copy-done.5
  10.0 83.1 %expert_layer.1 = bf16[64,3584]{1,0:T(8,128)(2,1)S(1)} custom-call(bf16[64,3584]{1,0:T(8,128)(2,1)S(1)} %copy-done.1, s32[64,2]{1,0:T(8,128)S(1)} %copy.13.ids, f32[64,2]{1,0:T(8,128)S(1)} %copy.14.wts, bf16[1,3584,512]{2,1,0:T(8,128)(2,1)S(1)} %copy-done, bf16[1,3584,512]{2,1,0:T(8,128)(2,1)} %up_w.1, bf16[1,512,3584]{2,1,0:T(8,128)(2,1)} %down_w.1, ...), custom_call_target="tpu_custom_call" | custom-call | flops 8589934592 | bytes 13631488 | tf_op jit(solution)/shard_map/expert_layer/pallas_call | solution.py:520
  93.1 0.8 copy.18
Async XLA Ops:
  3.9 2.0 %copy-start = (bf16[1,3584,512]{2,1,0:T(8,128)(2,1)S(1)}, bf16[1,3584,512]{2,1,0:T(8,128)(2,1)}, u32[]{:S(2)}) copy-start(bf16[1,3584,512]{2,1,0:T(8,128)(2,1)} %gate_w.1) | copy-start | bytes 11010052
  6.0 1.0 %copy-start.1 = (bf16[64,3584]{1,0:T(8,128)(2,1)S(1)}, bf16[64,3584]{1,0:T(8,128)(2,1)}, u32[]{:S(2)}) copy-start(bf16[64,3584]{1,0:T(8,128)(2,1)} %rows.1) | copy-start | bytes 1376260
  7.0 0.9 %copy-start.2 = (bf16[8,64,224]{2,1,0:T(8,128)(2,1)S(1)}, bf16[8,64,224]{2,1,0:T(8,128)(2,1)}, u32[]{:S(2)}) copy-start(bf16[8,64,224]{2,1,0:T(8,128)(2,1)} %down_a.1) | copy-start | bytes 688132
  7.9 0.7 copy-start.3
  8.6 0.7 copy-start.4
  9.3 0.7 copy-start.5

commit v2 on v1

--- a/solution.py
+++ b/solution.py
@@ -48,7 +48,7 @@
     rows, ids, wts, gate_w, up_w, down_w, gate_b, gate_a, up_b, up_a, down_b, down_a,
     out,
     rw, meta, tab, wtab, sel, got, w, dw, acc, low, hid, back, back_got,
-    pack_g, pack_u, pack_d, fac, gub, daf, dbf, a2,
+    ids_v, wts_v, ga_v, ua_v, db_v, pack_g, pack_u, pack_d, fac_a, fac_b, gub, daf, dbf, a2,
     zs, zr, own, fin, fin_got,
     s_load, s_w, s_dw, s_meta, s_zrow, r_zrow, r_meta,
     s_x, r_x, s_fwd, r_fwd, s_dwx, r_dwx, s_fac, r_facz, r_facy, r_facd,
@@ -70,7 +70,6 @@
     z_peers = [dev(y, (zl + d) % 4, x, zh, c) for d in (1, 2, 3)]
     y_peers = [dev((y + d) % 4, zl, x, zh, c) for d in (1, 2, 3)]
     far = jnp.where((zl == 1) | (zl == 2), 1, 0)
-    first, second = far, 1 - far
 
     def remote(src, dst, ssem, rsem, target):
         return pltpu.make_async_remote_copy(
@@ -81,16 +80,16 @@
         pltpu.make_async_copy(ref, ref, sem).wait()
 
     loads = [
-        pltpu.make_async_copy(gate_b.at[pair], pack_g, s_load.at[0]),
-        pltpu.make_async_copy(up_b.at[pair], pack_u, s_load.at[1]),
-        pltpu.make_async_copy(down_a.at[pair], pack_d, s_load.at[2]),
+        pltpu.make_async_copy(src, dst, s_load.at[NK + n]) for n, (src, dst) in enumerate((
+            (ids, ids_v), (wts, wts_v), (gate_b.at[pair], pack_g), (up_b.at[pair], pack_u),
+            (down_a.at[pair], pack_d), (gate_a, ga_v), (up_a, ua_v), (down_b, db_v)))
     ]
     for copy in loads:
         copy.start()
 
     def row_load(k):
         return pltpu.make_async_copy(
-            rows.at[:, pl.ds(pl.multiple_of(k * KC, KC), KC)], rw.at[0, k], s_load.at[3 + k])
+            rows.at[:, pl.ds(pl.multiple_of(k * KC, KC), KC)], rw.at[0, k], s_load.at[k])
 
     def w_load(k, part):
         src = (gate_w, up_w)[part]
@@ -121,12 +120,14 @@
     for peer in peers:
         pl.semaphore_signal(barrier, inc=1, device_id=peer, device_id_type=MESH)
 
-    lane = iota((ROWS, 128), 1)
-    idf = ids[...].astype(F32)
-    wt = wts[...]
-    meta[0, c] = jnp.where(
-        lane == 0, idf[:, 0:1],
-        jnp.where(lane == 1, idf[:, 1:2], jnp.where(lane == 2, wt[:, 0:1], wt[:, 1:2])))
+    loads[0].wait()
+    loads[1].wait()
+    line = iota((128, ROWS), 0)
+    idf = ids_v[...].astype(F32)
+    named = jnp.where(
+        line == 0, idf[0:1, :],
+        jnp.where(line == 1, idf[1:2, :], jnp.where(line == 2, wts_v[0:1, :], wts_v[1:2, :])))
+    meta[0, c] = named.T
 
     pl.semaphore_wait(barrier, len(peers))
 
@@ -140,49 +141,6 @@
         return remote(
             rows.at[:, pl.ds(pl.multiple_of(k * KC, KC), KC)], rw.at[1, k],
             s_zrow.at[k], r_zrow.at[k], mirror)
-
-    @pl.when(far == 0)
-    def _():
-        @pl.loop(0, NK)
-        def _(k):
-            zrow(k).start()
-
-    for copy in loads:
-        copy.wait()
-    half = pl.ds(pl.multiple_of(c * PART, 16), PART)
-    left64 = onehot(iota((64, 128), 0) == iota((64, 128), 1))
-    right64 = onehot(iota((64, 128), 0) + 64 == iota((64, 128), 1))
-    packed = dot(pack_g[half, :], left64) + dot(pack_u[half, :], right64)
-    mine = fac.at[y, zl, c]
-    mine[:, 0:128] = packed.astype(BF)
-    pick = onehot(iota((PART, SHARD), 1) == iota((PART, SHARD), 0) + c * PART)
-    turned = dot_nt(pick, pack_d[...]).astype(BF)
-    placed = dot(onehot(iota((PART, 32), 0) == iota((PART, 32), 1)), down_b[0]).astype(BF)
-    row = iota((PART, 4), 0) - 32
-    fits = (row >= 0) & (row < 64)
-    which = (row + 32) % 8
-    col = iota((PART, 4), 1)
-    spread = (dot(onehot(fits & (which == col)), gate_a[0])
-              + dot(onehot(fits & (which == col + 4)), up_a[0]))
-    block = (iota((PART, HID), 0) - 32) // 8
-    spread = jnp.where(block == iota((PART, HID), 1) // 64, spread, 0.0).astype(BF)
-    fold = onehot(iota((HID, 128), 0) % 64 + 64 == iota((HID, 128), 1))
-    packed = dot(turned, left64) + dot(placed, right64) + dot(spread, fold)
-    mine[:, 128:256] = packed.astype(BF)
-
-    for d in range(3):
-        remote(fac.at[y, zl, c], fac.at[y, zl, c], s_fac.at[0], r_facz, z_peers[d]).start()
-
-    @pl.when(far == 1)
-    def _():
-        @pl.loop(0, NK)
-        def _(k):
-            zrow(k).start()
-
-    @pl.loop(0, NJ)
-    def _(j):
-        dw_load(j).start()
-        dw_send(j).start()
 
     def tables(m):
         lane = iota((ROWS, 128), 1)
@@ -236,98 +194,88 @@
         value = got[om, k].reshape(8 * CAP, KC)
         for n in range(4):
             cols = pl.ds(n * 256, 256)
-            part = dot(value, w[k, :, cols])
-
-            @pl.when(k == 0)
-            def _():
-                acc[om, :, cols] = part
-
-            @pl.when(k > 0)
-            def _():
-                acc[om, :, cols] += part
-
-    make_select(0)
+            acc[om, :, cols] += dot(value, w[k, :, cols])
+
+    def low_part(om, k):
+        return dot(got[om, k].reshape(8 * CAP, KC),
+                   gub[pl.ds(pl.multiple_of(k * KC, KC), KC), :])
+
+    @pl.when(far == 0)
+    def _():
+        @pl.loop(0, NK)
+        def _(k):
+            zrow(k).start()
+
+    for copy in loads[2:]:
+        copy.wait()
+    left64 = onehot(iota((64, 128), 0) == iota((64, 128), 1))
+    right64 = onehot(iota((64, 128), 0) + 64 == iota((64, 128), 1))
+    pick = onehot(iota((PART, SHARD), 1) == iota((PART, SHARD), 0) + c * PART)
+    fac_a[y, zl, c, 0:PART, :] = (
+        dot(dot_nt(pick, pack_g[...]).astype(BF), left64)
+        + dot(dot_nt(pick, pack_u[...]).astype(BF), right64)).astype(BF)
+    rights = jnp.concatenate([ga_v[0].astype(F32), ua_v[0].astype(F32)], axis=0)
+    fac_a[y, zl, c, PART:PART + 32, :] = jnp.concatenate(
+        [rights[:, 128 * q:128 * q + 128] for q in range(4)], axis=0).astype(BF)
+
+    def fac_z(part):
+        fac = (fac_a, fac_b)[part]
+        for d in range(3):
+            remote(fac.at[y, zl, c], fac.at[y, zl, c],
+                   s_fac.at[part, 0], r_facz.at[part], z_peers[d]).start()
+
+    fac_z(0)
 
     @pl.when(far == 1)
     def _():
-        meta_mirror.wait_recv()
-        meta_second.start()
-        make_select(1)
-
-    @pl.loop(0, 3)
-    def _(k):
-        dispatch(first, k)
-
-    wait_bytes(fac.at[0, pl.ds(0, 3), 0], r_facz)
-    for d in range(3):
-        remote(fac.at[y, :, c], fac.at[y, :, c], s_fac.at[1], r_facy, y_peers[d]).start()
-
-    @pl.loop(3, NK)
-    def _(k):
-        dispatch(first, k)
-
-    @pl.when(far == 0)
-    def _():
-        meta_mirror.wait_recv()
-        meta_second.start()
-        make_select(1)
-
-    @pl.loop(0, NK + 1)
-    def _(k):
-        @pl.when(k < NK)
-        def _():
-            dispatch(second, k)
-            arrive(first, k)
-            w_load(k, 0).wait()
-            w_load(k, 1).wait()
-
-        @pl.when(k > 0)
-        def _():
-            gate_up(first, k - 1)
-
-    wait_bytes(fac.at[pl.ds(0, 3), :, 0], r_facy)
-    fac_forward = remote(fac.at[:, :, c], fac.at[:, :, c], s_fac.at[2], r_facd, sibling)
-    fac_forward.start()
-    meta_sibling.wait_recv()
-    meta_second.wait_recv()
-    make_weights(0, 1 - c)
-    make_weights(1, 1 - c)
-    fac_forward.wait_recv()
-
-    left = iota((896, 128), 1) < 64
-    for yy in range(4):
-        gub[pl.ds(yy * 896, 896), :] = fac[yy, :, :, :, 0:128].reshape(896, 128)
-        part = fac[yy, :, :, :, 128:256].reshape(896, 128).astype(F32)
-        part = jnp.where(left, part, 0.0)
-        daf[pl.ds(yy * 896, 896), :] = (part + pltpu.roll(part, 64, 1)).astype(BF)
-        for core in range(2):
-            part = fac[yy, :, core, 0:32, 128:256].reshape(128, 128)
-            dbf[core, pl.ds(yy * 128, 128), :] = jnp.where(
-                iota((128, 128), 1) < 64, jnp.zeros_like(part), part)
-    small = fac[:, :, c, 32:96, 128:256].reshape(1024, 128)
-    unfold = onehot((iota((128, HID), 1) % 64 + 64) == iota((128, HID), 0))
-    wide = dot(small, unfold)
-    block = (iota((1024, HID), 0) % 64) // 8
-    wide = jnp.where(block == iota((1024, HID), 1) // 64, wide, 0.0).astype(BF)
-    r = iota((128, 1024), 0)
-    s = iota((128, 1024), 1)
-    take = onehot((s // 64 == (r % 64) // 4) & (s % 8 == r % 4 + 4 * (r // 64)))
-    right = dot(take, wide).astype(BF)
-    upper = iota((128, HID), 0) < 64
-    for n in range(2):
-        rs = pl.ds(n * 128, 128)
-        a2[rs, 0:HID] = jnp.where(upper, right, jnp.zeros_like(right))
-        a2[rs, HID:2 * HID] = jnp.where(upper, jnp.zeros_like(right), right)
-
-    def hidden(om):
-        low[...] = jnp.zeros_like(low)
-
         @pl.loop(0, NK)
         def _(k):
-            low[...] += dot(got[om, k].reshape(8 * CAP, KC),
-                            gub[pl.ds(pl.multiple_of(k * KC, KC), KC), :])
-
-        high, rest = split(low[...])
+            zrow(k).start()
+
+    make_select(0)
+
+    @pl.loop(0, NK)
+    def _(k):
+        dispatch(0, k)
+
+    turned = dot_nt(pick, pack_d[...]).astype(BF)
+    placed = dot(onehot(iota((PART, 32), 0) == iota((PART, 32), 1)), db_v[0]).astype(BF)
+    fac_b[y, zl, c] = (dot(turned, left64) + dot(placed, right64)).astype(BF)
+    fac_z(1)
+
+    @pl.loop(0, NJ)
+    def _(j):
+        dw_load(j).start()
+        dw_send(j).start()
+
+    acc[...] = jnp.zeros_like(acc)
+    low[...] = jnp.zeros_like(low)
+
+    def fac_forward(part, yy):
+        fac = (fac_a, fac_b)[part]
+        return remote(fac.at[yy, :, c], fac.at[yy, :, c],
+                      s_fac.at[part, 2], r_facd.at[part, (yy - y + 4) % 4], sibling)
+
+    def fac_y(part):
+        fac = (fac_a, fac_b)[part]
+        wait_bytes(fac.at[0, pl.ds(0, 3), 0], r_facz.at[part])
+        for d in range(3):
+            remote(fac.at[y, :, c], fac.at[y, :, c],
+                   s_fac.at[part, 1], r_facy.at[part, d], y_peers[d]).start()
+        fac_forward(part, y).start()
+
+    def fac_cross(part):
+        fac = (fac_a, fac_b)[part]
+        for d in range(3):
+            wait_bytes(fac.at[0, :, 0], r_facy.at[part, d])
+            fac_forward(part, (y + 3 - d) % 4).start()
+
+    def fac_arrive(part):
+        for d in range(4):
+            fac_forward(part, (y + d) % 4).wait_recv()
+
+    def hidden(om, value):
+        high, rest = split(value)
         both = jnp.concatenate([high, rest], axis=1)
         for n in range(2):
             cols, ups = pl.ds(n * 256, 256), pl.ds(HID + n * 256, 256)
@@ -387,48 +335,123 @@
         cols = pl.ds(pl.multiple_of(c * HALF + j * JC, JC), JC)
         out[:, cols] = (own[j, c] + zr[j, c].astype(F32)).astype(BF)
 
-    hidden(first)
-
-    @pl.loop(0, NJ)
-    def _(j):
-        dw_load(j).wait()
-        dw_send(j).wait_recv()
-
-    low_first = low_down(first)
+    fac_y(0)
 
     @pl.loop(0, NK + 1)
     def _(k):
         @pl.when(k < NK)
         def _():
-            arrive(second, k)
-            down(first, k, low_first)
-
-        @pl.when(k > 0)
-        def _():
-            gate_up(second, k - 1)
-
-    hidden(second)
-
-    @pl.loop(0, 3)
-    def _(j):
-        combine(first, j)
-
-    low_second = low_down(second)
-
-    @pl.loop(0, NJ)
-    def _(j):
-        down(second, j, low_second)
-
-        @pl.when(j + 3 < NJ)
-        def _():
-            combine(first, j + 3)
-
-    @pl.loop(0, NJ)
-    def _(j):
-        combine(second, j)
-
-    @pl.loop(0, NJ)
-    def _(j):
+            arrive(0, k)
+
+        @pl.when(k == 3)
+        def _():
+            meta_mirror.wait_recv()
+            meta_second.start()
+            make_select(1)
+
+        @pl.when((far == 1) & (k == 4))
+        def _():
+            fac_y(1)
+
+        @pl.when(k >= 1)
+        def _():
+            w_load(k - 1, 0).wait()
+            w_load(k - 1, 1).wait()
+            gate_up(0, k - 1)
+
+        @pl.when((far == 1) & (k >= 4) & (k < NK))
+        def _():
+            dispatch(1, k - 4)
+
+    @pl.when(far == 0)
+    def _():
+        @pl.loop(0, 3)
+        def _(k):
+            dispatch(1, k)
+
+        fac_y(1)
+
+    meta_sibling.wait_recv()
+    make_weights(0, 1 - c)
+    meta_second.wait_recv()
+    make_weights(1, 1 - c)
+
+    @pl.loop(3, NK)
+    def _(k):
+        dispatch(1, k)
+        arrive(1, k - 3)
+
+        @pl.when(k >= 4)
+        def _():
+            gate_up(1, k - 4)
+
+        @pl.when(k == 4)
+        def _():
+            fac_cross(0)
+
+    fac_arrive(0)
+    for yy in range(4):
+        gub[pl.ds(yy * 896, 896), :] = fac_a[yy, :, :, 0:PART, :].reshape(896, 128)
+    small = fac_a[:, :, c, PART:PART + 32, :].astype(F32).reshape(16, 4, 8, 128)
+    r = iota((128, 128), 0)
+    s = iota((128, 128), 1)
+    take = onehot((s // 8 == (r % 64) // 4) & (s % 8 == r % 4 + 4 * (r // 64)))
+    upper = r < 64
+    for q in range(4):
+        right = dot(take, small[:, q].reshape(128, 128).astype(BF)).astype(BF)
+        none = jnp.zeros_like(right)
+        for n in range(2):
+            rs = pl.ds(n * 128, 128)
+            a2[rs, pl.ds(128 * q, 128)] = jnp.where(upper, right, none)
+            a2[rs, pl.ds(HID + 128 * q, 128)] = jnp.where(upper, none, right)
+    hidden(0, sum(low_part(0, k) for k in range(NK)))
+    fac_cross(1)
+    arrive(1, 4)
+    gate_up(1, 3)
+    fac_arrive(1)
+    left = iota((896, 128), 1) < 64
+    for yy in range(4):
+        part = fac_b[yy].reshape(896, 128).astype(F32)
+        part = jnp.where(left, part, 0.0)
+        daf[pl.ds(yy * 896, 896), :] = (part + pltpu.roll(part, 64, 1)).astype(BF)
+        for core in range(2):
+            part = fac_b[yy, :, core, 0:32, :].reshape(128, 128)
+            dbf[core, pl.ds(yy * 128, 128), :] = jnp.where(
+                iota((128, 128), 1) < 64, jnp.zeros_like(part), part)
+
+    @pl.loop(0, NJ)
+    def _(j):
+        dw_load(j).wait()
+        dw_send(j).wait_recv()
+
+    low_own = low_down(0)
+    down(0, 0, low_own)
+    arrive(1, 5)
+    down(0, 1, low_own)
+    gate_up(1, 4)
+    low[...] = sum(low_part(1, k) for k in range(5))
+    arrive(1, 6)
+    down(0, 2, low_own)
+    gate_up(1, 5)
+    gate_up(1, 6)
+    hidden(1, low[...] + low_part(1, 5) + low_part(1, 6))
+    low_mirror = low_down(1)
+
+    @pl.loop(0, NJ)
+    def _(j):
+        down(1, j, low_mirror)
+
+    @pl.loop(3, NJ)
+    def _(j):
+        down(0, j, low_own)
+
+    @pl.loop(0, NJ)
+    def _(j):
+        combine(1, j)
+
+    @pl.loop(0, NJ)
+    def _(j):
+        combine(0, j)
         finish(j)
 
     @pl.loop(0, NJ)
@@ -442,9 +465,10 @@
     meta_second.wait_send()
     wait_bytes(sel, s_x)
     wait_bytes(back, s_ret)
-    wait_bytes(fac.at[0, pl.ds(0, 3), 0], s_fac.at[0])
-    wait_bytes(fac.at[pl.ds(0, 3), :, 0], s_fac.at[1])
-    fac_forward.wait_send()
+    for part, fac in enumerate((fac_a, fac_b)):
+        wait_bytes(fac.at[0, pl.ds(0, 3), 0], s_fac.at[part, 0])
+        wait_bytes(fac.at[pl.ds(0, 3), :, 0], s_fac.at[part, 1])
+        wait_bytes(fac.at[:, :, 0], s_fac.at[part, 2])
     for om in range(2):
         hid_send(om).wait_send()
 
@@ -460,9 +484,11 @@
         fin_send(j).wait_send()
 
 
-def on_device(*args):
+def on_device(rows, ids, wts, gate_w, up_w, down_w, gate_b, gate_a, up_b, up_a, down_b, down_a):
+    args = (rows, ids.T, wts.T, gate_w, up_w, down_w, gate_b.swapaxes(1, 2), gate_a,
+            up_b.swapaxes(1, 2), up_a, down_b, down_a)
     vmem = pl.BlockSpec(memory_space=pltpu.VMEM)
-    hbm = pl.BlockSpec(memory_space=pl.ANY)
+    hbm = pl.BlockSpec(memory_space=pltpu.HBM)
     dma = pltpu.SemaphoreType.DMA
     scratch = [
         pltpu.VMEM((2, NK, ROWS, KC), BF),
@@ -478,10 +504,16 @@
         pltpu.VMEM((2, 2, 8 * CAP, HID), BF),
         pltpu.VMEM((2, NJ, 3, 2, CAP, JC), BF),
         pltpu.VMEM((2, NJ, 4, 2, CAP, JC), BF),
-        pltpu.VMEM((SHARD, RANK), BF),
-        pltpu.VMEM((SHARD, RANK), BF),
+        pltpu.VMEM((2, ROWS), jnp.int32),
+        pltpu.VMEM((2, ROWS), F32),
+        pltpu.VMEM((1, 4, HID), BF),
+        pltpu.VMEM((1, 4, HID), BF),
+        pltpu.VMEM((1, 32, RANK), BF),
         pltpu.VMEM((RANK, SHARD), BF),
-        pltpu.VMEM((4, 4, 2, PART, 256), BF),
+        pltpu.VMEM((RANK, SHARD), BF),
+        pltpu.VMEM((RANK, SHARD), BF),
+        pltpu.VMEM((4, 4, 2, PART + 32, 128), BF),
+        pltpu.VMEM((4, 4, 2, PART, 128), BF),
         pltpu.VMEM((D, 128), BF),
         pltpu.VMEM((D, 128), BF),
         pltpu.VMEM((2, HID, 128), BF),
@@ -491,7 +523,7 @@
         pltpu.VMEM((NJ, 2, ROWS, JC), F32),
         pltpu.VMEM((NJ, ROWS, JC), BF),
         pltpu.VMEM((NJ, ROWS, JC), BF),
-        dma((3 + NK,)),
+        dma((NK + 8,)),
         dma((NK, 2)),
         dma((NJ,)),
         dma((3,)),
@@ -504,10 +536,10 @@
         dma((2, NK)),
         dma((NJ,)),
         dma((NJ,)),
-        dma((3,)),
-        dma,
-        dma,
-        dma,
+        dma((2, 3)),
+        dma((2,)),
+        dma((2, 3)),
+        dma((2, 4)),
         dma((2,)),
         dma((2,)),
         dma,
@@ -520,11 +552,11 @@
     return pl.pallas_call(
         kernel,
         out_shape=jax.ShapeDtypeStruct((ROWS, D), BF),
-        in_specs=[hbm, vmem, vmem, hbm, hbm, hbm, hbm, vmem, hbm, vmem, vmem, hbm],
+        in_specs=[hbm] * 12,
         out_specs=vmem,
         scratch_shapes=scratch,
         compiler_params=pltpu.CompilerParams(
-            collective_id=0, has_side_effects=True, vmem_limit_bytes=48 << 20),
+            collective_id=0, has_side_effects=True, vmem_limit_bytes=63 << 20),
         cost_estimate=pl.CostEstimate(
             flops=8 << 30, bytes_accessed=13 << 20, transcendentals=1 << 18),
         name="expert_layer",

time: 94.2 us -> 75.1 us (0.80)
  Pallas kernels: 83.1 us -> 73.1 us
  local copies, waits for them, and re-layouts: 10.8 us -> 1.82 us
    pallas_call x1, Pallas kernels: 83.1 us -> 73.1 us  [on_device(): pl.pallas_call(kernel, out_shape=jax.ShapeDtypeStruct((ROWS, D), BF), in_...]
    unnamed x17 -> x1, local copies, waits for them, and re-layouts: 10.8 us -> 1.82 us
where the time goes in v2:
time: 75.1 us; the launch traced here: 75 us
  Pallas kernels  73.1 us (97%)
  local copies, waits for them, and re-layouts  1.82 us (2%)
    pallas_call x1, Pallas kernels, on_device(): pl.pallas_call(kernel, out_shape=jax.ShapeDtypeStruct((ROWS, D), BF), in_...  73.1 us
    unnamed x1, local copies, waits for them, and re-layouts  1.82 us

profile of v2, /device:TPU:1, one launch (start us, length us, event | category | flops | bytes accessed | tf_op | source)
XLA Modules:
  0.0 75.0 jit_solution(16788660026163129875)
XLA Ops:
  0.0 73.1 %expert_layer.1 = bf16[64,3584]{1,0:T(8,128)(2,1)} custom-call(bf16[64,3584]{1,0:T(8,128)(2,1)} %rows.1, s32[2,64]{1,0:T(2,128)} %bitcast.6, f32[2,64]{1,0:T(2,128)} %bitcast.7, bf16[1,3584,512]{2,1,0:T(8,128)(2,1)} %gate_w.1, bf16[1,3584,512]{2,1,0:T(8,128)(2,1)} %up_w.1, bf16[1,512,3584]{2,1,0:T(8,128)(2,1)} %down_w.1, bf16[8,64,224]{2,1,0:T(8,128)(2,1)} %bitcast.4, ...), custom_call_target="tpu_custom_call" | custom-call | flops 8589934592 | bytes 13631488 | tf_op jit(solution)/shard_map/expert_layer/pallas_call | solution.py:552
  73.2 1.8 %copy.14 = bf16[64,3584]{1,0:T(8,128)(2,1)} copy(bf16[64,3584]{1,0:T(8,128)(2,1)} %expert_layer.1) | data formatting | bytes 917504

commit v3 on v2

--- a/solution.py
+++ b/solution.py
@@ -47,7 +47,7 @@
 def kernel(
     rows, ids, wts, gate_w, up_w, down_w, gate_b, gate_a, up_b, up_a, down_b, down_a,
     out,
-    rw, meta, tab, wtab, sel, got, w, dw, acc, low, hid, back, back_got,
+    rw, meta, tab, wtab, sel, got, w, dw, acc, hid, back, back_got,
     ids_v, wts_v, ga_v, ua_v, db_v, pack_g, pack_u, pack_d, fac_a, fac_b, gub, daf, dbf, a2,
     zs, zr, own, fin, fin_got,
     s_load, s_w, s_dw, s_meta, s_zrow, r_zrow, r_meta,
@@ -189,22 +189,38 @@
         wait_bytes(sel.at[om, k], r_x.at[om, k])
         forward(om, k).start()
 
-    def gate_up(om, k):
-        forward(om, k).wait_recv()
-        value = got[om, k].reshape(8 * CAP, KC)
+    def span(st):
+        return pl.ds(0, 8 * CAP) if st == 0 else pl.ds((st - 1) * 4 * CAP, 4 * CAP)
+
+    def chosen(st, k):
+        if st == 0:
+            return got[0, k].reshape(8 * CAP, KC)
+        return got[1, k, :, st - 1].reshape(4 * CAP, KC)
+
+    def gate_up(st, k):
+        om, rs = min(st, 1), span(st)
+        if st == 0:
+            forward(0, k).wait_recv()
+        else:
+            @pl.when(c == 2 - st)
+            def _():
+                forward(1, k).wait_recv()
+        value = chosen(st, k)
         for n in range(4):
             cols = pl.ds(n * 256, 256)
-            acc[om, :, cols] += dot(value, w[k, :, cols])
-
-    def low_part(om, k):
-        return dot(got[om, k].reshape(8 * CAP, KC),
-                   gub[pl.ds(pl.multiple_of(k * KC, KC), KC), :])
-
-    @pl.when(far == 0)
-    def _():
+            acc[om, rs, cols] += dot(value, w[k, :, cols])
+
+    def low_rank(st):
+        return sum(dot(chosen(st, k), gub[pl.ds(k * KC, KC), :]) for k in range(NK))
+
+    def zrow_start():
         @pl.loop(0, NK)
         def _(k):
             zrow(k).start()
+
+    @pl.when((far == 0) & (c == 0))
+    def _():
+        zrow_start()
 
     for copy in loads[2:]:
         copy.wait()
@@ -218,19 +234,24 @@
     fac_a[y, zl, c, PART:PART + 32, :] = jnp.concatenate(
         [rights[:, 128 * q:128 * q + 128] for q in range(4)], axis=0).astype(BF)
 
+    def fac_y_send(part, zz):
+        fac = (fac_a, fac_b)[part]
+        for d in range(3):
+            remote(fac.at[y, zz, c], fac.at[y, zz, c],
+                   s_fac.at[part, 1], r_facy.at[part, d], y_peers[d]).start()
+
     def fac_z(part):
         fac = (fac_a, fac_b)[part]
         for d in range(3):
             remote(fac.at[y, zl, c], fac.at[y, zl, c],
-                   s_fac.at[part, 0], r_facz.at[part], z_peers[d]).start()
+                   s_fac.at[part, 0], r_facz.at[part, d], z_peers[d]).start()
+        fac_y_send(part, zl)
 
     fac_z(0)
 
-    @pl.when(far == 1)
-    def _():
-        @pl.loop(0, NK)
-        def _(k):
-            zrow(k).start()
+    @pl.when((far == 1) & (c == 0))
+    def _():
+        zrow_start()
 
     make_select(0)
 
@@ -249,7 +270,6 @@
         dw_send(j).start()
 
     acc[...] = jnp.zeros_like(acc)
-    low[...] = jnp.zeros_like(low)
 
     def fac_forward(part, yy):
         fac = (fac_a, fac_b)[part]
@@ -258,10 +278,9 @@
 
     def fac_y(part):
         fac = (fac_a, fac_b)[part]
-        wait_bytes(fac.at[0, pl.ds(0, 3), 0], r_facz.at[part])
         for d in range(3):
-            remote(fac.at[y, :, c], fac.at[y, :, c],
-                   s_fac.at[part, 1], r_facy.at[part, d], y_peers[d]).start()
+            wait_bytes(fac.at[0, 0, 0], r_facz.at[part, d])
+            fac_y_send(part, (zl + 3 - d) % 4)
         fac_forward(part, y).start()
 
     def fac_cross(part):
@@ -274,62 +293,72 @@
         for d in range(4):
             fac_forward(part, (y + d) % 4).wait_recv()
 
-    def hidden(om, value):
-        high, rest = split(value)
+    def hidden(st):
+        om, rs = min(st, 1), span(st)
+        high, rest = split(low_rank(st))
         both = jnp.concatenate([high, rest], axis=1)
         for n in range(2):
             cols, ups = pl.ds(n * 256, 256), pl.ds(HID + n * 256, 256)
-            gate = acc[om, :, cols] + dot(both, a2[:, cols])
-            up = acc[om, :, ups] + dot(both, a2[:, ups])
-            hid[om, c, :, cols] = (gate / (1.0 + jnp.exp(-gate)) * up).astype(BF)
-        hid_send(om).start()
-
-    def hid_send(om):
-        return remote(hid.at[om, c], hid.at[om, c], s_hid.at[om], r_hid.at[om], sibling)
-
-    def low_down(om):
-        hid_send(om).wait_recv()
-        value = dot(hid[om, 0], dbf[0]) + dot(hid[om, 1], dbf[1])
+            gate = acc[om, rs, cols] + dot(both, a2[:, cols])
+            up = acc[om, rs, ups] + dot(both, a2[:, ups])
+            hid[om, c, rs, cols] = (gate / (1.0 + jnp.exp(-gate)) * up).astype(BF)
+        hid_send(st).start()
+
+    def hid_send(st):
+        part = hid.at[min(st, 1), c, span(st)]
+        return remote(part, part, s_hid.at[st], r_hid.at[st], sibling)
+
+    def low_down(st):
+        om, rs = min(st, 1), span(st)
+        hid_send(st).wait_recv()
+        value = dot(hid[om, 0, rs], dbf[0]) + dot(hid[om, 1, rs], dbf[1])
         high, rest = split(value)
         low2 = high.astype(F32) + pltpu.roll(rest.astype(F32), 64, 1)
         return low2.astype(BF)
 
-    def down(om, j, low2):
+    def down(st, j, low2):
+        om, rs = min(st, 1), span(st)
         da = daf[pl.ds(pl.multiple_of(c * HALF + j * JC, JC), JC), :]
-        value = dot(hid[om, 0], dw[0, j]) + dot(hid[om, 1], dw[1, j]) + dot_nt(low2, da)
-        value = value.astype(BF).reshape(4, 2, CAP, JC)
-        back_got[om, j, 0] = value[0]
-        back[om, j] = value[1:]
+        value = dot(hid[om, 0, rs], dw[0, j]) + dot(hid[om, 1, rs], dw[1, j]) + dot_nt(low2, da)
+        value = value.astype(BF)
+        if st == 0:
+            value = value.reshape(4, 2, CAP, JC)
+            back_got[0, j, 0] = value[0]
+            back[0, j] = value[1:]
+        else:
+            value = value.reshape(4, CAP, JC)
+            back_got[1, j, 0, st - 1] = value[0]
+            back[1, j, :, st - 1] = value[1:]
         for d in range(3):
-            remote(back.at[om, j, d], back_got.at[om, j, d + 1],
-                   s_ret, r_ret.at[om, j], x_down[d]).start()
-
-    def zret(j):
-        return remote(zs.at[j], zr.at[j], s_zret.at[j], r_zret.at[j], mirror)
-
-    def combine(om, j):
-        wait_bytes(back.at[om, j], r_ret.at[om, j])
-        for cs in range(2):
-            value = dot(wtab[om, cs], back_got[om, j, :, cs].reshape(4 * CAP, JC))
-            value = value[0:ROWS] + value[ROWS:]
-
-            @pl.when(om == 0)
-            def _():
-                own[j, cs] = value
-
-            @pl.when(om == 1)
-            def _():
-                zs[j, cs] = value.astype(BF)
-
-        @pl.when(om == 1)
-        def _():
-            zret(j).start()
+            if st == 0:
+                src, dst = back.at[0, j, d], back_got.at[0, j, d + 1]
+            else:
+                src, dst = back.at[1, j, d, st - 1], back_got.at[1, j, d + 1, st - 1]
+            remote(src, dst, s_ret, r_ret.at[st, j], x_down[d]).start()
+
+    def zret(m, j):
+        return remote(zs.at[j, m], zr.at[j, m], s_zret.at[m, j], r_zret.at[m, j], mirror)
+
+    def mix(om, cs, j):
+        value = dot(wtab[om, cs], back_got[om, j, :, cs].reshape(4 * CAP, JC))
+        return value[0:ROWS] + value[ROWS:]
+
+    def combine(st, j):
+        if st == 0:
+            wait_bytes(back.at[0, j], r_ret.at[0, j])
+            for cs in range(2):
+                own[j, cs] = mix(0, cs, j)
+        else:
+            wait_bytes(back.at[1, j, :, st - 1], r_ret.at[st, j])
+            zs[j, st - 1] = mix(1, st - 1, j).astype(BF)
+            zret(st - 1, j).start()
 
     def fin_send(j):
         return remote(fin.at[j], fin_got.at[j], s_fin.at[j], r_fin.at[j], sibling)
 
     def finish(j):
-        zret(j).wait_recv()
+        zret(0, j).wait_recv()
+        zret(1, j).wait_recv()
         fin[j] = (own[j, 1 - c] + zr[j, 1 - c].astype(F32)).astype(BF)
         fin_send(j).start()
         cols = pl.ds(pl.multiple_of(c * HALF + j * JC, JC), JC)
@@ -337,11 +366,15 @@
 
     fac_y(0)
 
-    @pl.loop(0, NK + 1)
+    @pl.loop(0, NK + 2)
     def _(k):
         @pl.when(k < NK)
         def _():
             arrive(0, k)
+
+        @pl.when(((far == 1) & (c == 1) & (k == 4)) | ((far == 0) & (c == 1) & (k == 6)))
+        def _():
+            zrow_start()
 
         @pl.when(k == 3)
         def _():
@@ -349,45 +382,46 @@
             meta_second.start()
             make_select(1)
 
-        @pl.when((far == 1) & (k == 4))
+        @pl.when((far == 1) & (k == 3))
         def _():
             fac_y(1)
 
-        @pl.when(k >= 1)
-        def _():
-            w_load(k - 1, 0).wait()
-            w_load(k - 1, 1).wait()
-            gate_up(0, k - 1)
-
-        @pl.when((far == 1) & (k >= 4) & (k < NK))
-        def _():
-            dispatch(1, k - 4)
+        @pl.when((far == 1) & (c == 0) & (k >= 3) & (k < NK))
+        def _():
+            dispatch(1, 2 * k - 6)
+
+            @pl.when(k < NK - 1)
+            def _():
+                dispatch(1, 2 * k - 5)
+
+        @pl.when(k >= 2)
+        def _():
+            w_load(k - 2, 0).wait()
+            w_load(k - 2, 1).wait()
+            gate_up(0, k - 2)
+
+    fac_cross(0)
 
     @pl.when(far == 0)
     def _():
-        @pl.loop(0, 3)
+        fac_y(1)
+
+    @pl.when((far == 0) & (c == 0))
+    def _():
+        @pl.loop(0, NK)
         def _(k):
             dispatch(1, k)
-
-        fac_y(1)
 
     meta_sibling.wait_recv()
     make_weights(0, 1 - c)
     meta_second.wait_recv()
     make_weights(1, 1 - c)
 
-    @pl.loop(3, NK)
-    def _(k):
-        dispatch(1, k)
-        arrive(1, k - 3)
-
-        @pl.when(k >= 4)
-        def _():
-            gate_up(1, k - 4)
-
-        @pl.when(k == 4)
-        def _():
-            fac_cross(0)
+    @pl.when((far == 1) & (c == 1))
+    def _():
+        @pl.loop(0, 4)
+        def _(k):
+            dispatch(1, k)
 
     fac_arrive(0)
     for yy in range(4):
@@ -404,10 +438,40 @@
             rs = pl.ds(n * 128, 128)
             a2[rs, pl.ds(128 * q, 128)] = jnp.where(upper, right, none)
             a2[rs, pl.ds(HID + 128 * q, 128)] = jnp.where(upper, none, right)
-    hidden(0, sum(low_part(0, k) for k in range(NK)))
-    fac_cross(1)
-    arrive(1, 4)
-    gate_up(1, 3)
+    @pl.when(far == 0)
+    def _():
+        hidden(0)
+
+    @pl.when((far == 1) & (c == 1))
+    def _():
+        @pl.loop(4, NK)
+        def _(k):
+            dispatch(1, k)
+
+    @pl.loop(0, NK + 1)
+    def _(k):
+        @pl.when((c == 0) & (k < NK))
+        def _():
+            arrive(1, k)
+
+        @pl.when((far == 0) & (c == 1) & (k < NK))
+        def _():
+            dispatch(1, k)
+
+        @pl.when(k == 5)
+        def _():
+            fac_cross(1)
+
+        @pl.when(k > 0)
+        def _():
+            gate_up(1, k - 1)
+
+    hidden(1)
+
+    @pl.when(far == 1)
+    def _():
+        hidden(0)
+
     fac_arrive(1)
     left = iota((896, 128), 1) < 64
     for yy in range(4):
@@ -419,35 +483,79 @@
             dbf[core, pl.ds(yy * 128, 128), :] = jnp.where(
                 iota((128, 128), 1) < 64, jnp.zeros_like(part), part)
 
+
     @pl.loop(0, NJ)
     def _(j):
         dw_load(j).wait()
         dw_send(j).wait_recv()
 
+    low_a = low_down(1)
+
+    @pl.loop(0, NJ)
+    def _(j):
+        down(1, j, low_a)
+
     low_own = low_down(0)
     down(0, 0, low_own)
-    arrive(1, 5)
     down(0, 1, low_own)
-    gate_up(1, 4)
-    low[...] = sum(low_part(1, k) for k in range(5))
-    arrive(1, 6)
-    down(0, 2, low_own)
-    gate_up(1, 5)
-    gate_up(1, 6)
-    hidden(1, low[...] + low_part(1, 5) + low_part(1, 6))
-    low_mirror = low_down(1)
-
-    @pl.loop(0, NJ)
-    def _(j):
-        down(1, j, low_mirror)
-
-    @pl.loop(3, NJ)
+
+    @pl.when(far == 1)
+    def _():
+        @pl.when(c == 1)
+        def _():
+            @pl.loop(0, NK)
+            def _(k):
+                arrive(1, k)
+
+        combine(1, 0)
+        combine(1, 1)
+
+        @pl.loop(0, NK)
+        def _(k):
+            @pl.when(c == 0)
+            def _():
+                forward(1, k).wait_recv()
+
+        rs = span(2)
+        for n in range(4):
+            cols = pl.ds(n * 256, 256)
+            acc[1, rs, cols] = sum(dot(chosen(2, k), w[k, :, cols]) for k in range(NK))
+
+    @pl.when(far == 0)
+    def _():
+        @pl.loop(0, NK + 1)
+        def _(k):
+            @pl.when((c == 1) & (k < NK))
+            def _():
+                arrive(1, k)
+
+            @pl.when(k > 0)
+            def _():
+                gate_up(2, k - 1)
+
+            @pl.when(k >= NK - 1)
+            def _():
+                combine(1, k - NK + 1)
+
+    hidden(2)
+    combine(1, 2)
+    low_b = low_down(2)
+
+    @pl.loop(0, NJ)
+    def _(j):
+        down(2, j, low_b)
+
+        @pl.when(j < NJ - 3)
+        def _():
+            combine(1, j + 3)
+
+    @pl.loop(2, NJ)
     def _(j):
         down(0, j, low_own)
 
     @pl.loop(0, NJ)
     def _(j):
-        combine(1, j)
+        combine(2, j)
 
     @pl.loop(0, NJ)
     def _(j):
@@ -469,8 +577,9 @@
         wait_bytes(fac.at[0, pl.ds(0, 3), 0], s_fac.at[part, 0])
         wait_bytes(fac.at[pl.ds(0, 3), :, 0], s_fac.at[part, 1])
         wait_bytes(fac.at[:, :, 0], s_fac.at[part, 2])
+    for st in range(3):
+        hid_send(st).wait_send()
     for om in range(2):
-        hid_send(om).wait_send()
 
         @pl.loop(0, NK)
         def _(k):
@@ -480,7 +589,8 @@
     def _(j):
         zrow(j).wait_send()
         dw_send(j).wait_send()
-        zret(j).wait_send()
+        zret(0, j).wait_send()
+        zret(1, j).wait_send()
         fin_send(j).wait_send()
 
 
@@ -500,7 +610,6 @@
         pltpu.VMEM((NK, KC, 2 * HID), BF),
         pltpu.VMEM((2, NJ, HID, JC), BF),
         pltpu.VMEM((2, 8 * CAP, 2 * HID), F32),
-        pltpu.VMEM((8 * CAP, 128), F32),
         pltpu.VMEM((2, 2, 8 * CAP, HID), BF),
         pltpu.VMEM((2, NJ, 3, 2, CAP, JC), BF),
         pltpu.VMEM((2, NJ, 4, 2, CAP, JC), BF),
@@ -537,15 +646,15 @@
         dma((NJ,)),
         dma((NJ,)),
         dma((2, 3)),
-        dma((2,)),
+        dma((2, 3)),
         dma((2, 3)),
         dma((2, 4)),
-        dma((2,)),
-        dma((2,)),
+        dma((3,)),
+        dma((3,)),
         dma,
+        dma((3, NJ)),
         dma((2, NJ)),
-        dma((NJ,)),
-        dma((NJ,)),
+        dma((2, NJ)),
         dma((NJ,)),
         dma((NJ,)),
     ]

time: 75.1 us -> 67.3 us (0.90)
  Pallas kernels: 73.1 us -> 65.4 us
    pallas_call x1, Pallas kernels: 73.1 us -> 65.4 us  [on_device(): pl.pallas_call(kernel, out_shape=jax.ShapeDtypeStruct((ROWS, D), BF), in_...]
where the time goes in v3:
time: 67.3 us; the launch traced here: 67.2 us
  Pallas kernels  65.4 us (97%)
  local copies, waits for them, and re-layouts  1.82 us (3%)
    pallas_call x1, Pallas kernels, on_device(): pl.pallas_call(kernel, out_shape=jax.ShapeDtypeStruct((ROWS, D), BF), in_...  65.4 us
    unnamed x1, local copies, waits for them, and re-layouts  1.82 us

profile of v3, /device:TPU:1, one launch (start us, length us, event | category | flops | bytes accessed | tf_op | source)
XLA Modules:
  0.0 67.2 jit_solution(1393009381987607596)
XLA Ops:
  0.0 65.4 %expert_layer.1 = bf16[64,3584]{1,0:T(8,128)(2,1)} custom-call(bf16[64,3584]{1,0:T(8,128)(2,1)} %rows.1, s32[2,64]{1,0:T(2,128)} %bitcast.6, f32[2,64]{1,0:T(2,128)} %bitcast.7, bf16[1,3584,512]{2,1,0:T(8,128)(2,1)} %gate_w.1, bf16[1,3584,512]{2,1,0:T(8,128)(2,1)} %up_w.1, bf16[1,512,3584]{2,1,0:T(8,128)(2,1)} %down_w.1, bf16[8,64,224]{2,1,0:T(8,128)(2,1)} %bitcast.4, ...), custom_call_target="tpu_custom_call" | custom-call | flops 8589934592 | bytes 13631488 | tf_op jit(solution)/shard_map/expert_layer/pallas_call | solution.py:661
  65.4 1.8 %copy.14 = bf16[64,3584]{1,0:T(8,128)(2,1)} copy(bf16[64,3584]{1,0:T(8,128)(2,1)} %expert_layer.1) | data formatting | bytes 917504

commit v4 on v3

--- a/solution.py
+++ b/solution.py
@@ -248,10 +248,6 @@
         fac_y_send(part, zl)
 
     fac_z(0)
-
-    @pl.when((far == 1) & (c == 0))
-    def _():
-        zrow_start()
 
     make_select(0)
 
@@ -364,6 +360,10 @@
         cols = pl.ds(pl.multiple_of(c * HALF + j * JC, JC), JC)
         out[:, cols] = (own[j, c] + zr[j, c].astype(F32)).astype(BF)
 
+    @pl.when((far == 1) & (c == 0))
+    def _():
+        zrow_start()
+
     fac_y(0)
 
     @pl.loop(0, NK + 2)
@@ -372,21 +372,21 @@
         def _():
             arrive(0, k)
 
-        @pl.when(((far == 1) & (c == 1) & (k == 4)) | ((far == 0) & (c == 1) & (k == 6)))
+        @pl.when((c == 1) & (k == jnp.where(far == 1, 6, 5)))
         def _():
             zrow_start()
 
-        @pl.when(k == 3)
+        @pl.when(k == 2)
         def _():
             meta_mirror.wait_recv()
             meta_second.start()
             make_select(1)
 
-        @pl.when((far == 1) & (k == 3))
+        @pl.when(k == 4 - far)
         def _():
             fac_y(1)
 
-        @pl.when((far == 1) & (c == 0) & (k >= 3) & (k < NK))
+        @pl.when((c == 0) & (k >= 3) & (k < NK))
         def _():
             dispatch(1, 2 * k - 6)
 
@@ -401,16 +401,6 @@
             gate_up(0, k - 2)
 
     fac_cross(0)
-
-    @pl.when(far == 0)
-    def _():
-        fac_y(1)
-
-    @pl.when((far == 0) & (c == 0))
-    def _():
-        @pl.loop(0, NK)
-        def _(k):
-            dispatch(1, k)
 
     meta_sibling.wait_recv()
     make_weights(0, 1 - c)
@@ -442,6 +432,12 @@
     def _():
         hidden(0)
 
+        @pl.when(c == 1)
+        def _():
+            @pl.loop(0, NK)
+            def _(k):
+                dispatch(1, k)
+
     @pl.when((far == 1) & (c == 1))
     def _():
         @pl.loop(4, NK)
@@ -453,10 +449,6 @@
         @pl.when((c == 0) & (k < NK))
         def _():
             arrive(1, k)
-
-        @pl.when((far == 0) & (c == 1) & (k < NK))
-        def _():
-            dispatch(1, k)
 
         @pl.when(k == 5)
         def _():
@@ -495,49 +487,37 @@
     def _(j):
         down(1, j, low_a)
 
+    @pl.when(c == 1)
+    def _():
+        @pl.loop(0, NK)
+        def _(k):
+            arrive(1, k)
+
     low_own = low_down(0)
     down(0, 0, low_own)
     down(0, 1, low_own)
 
     @pl.when(far == 1)
     def _():
-        @pl.when(c == 1)
-        def _():
-            @pl.loop(0, NK)
-            def _(k):
-                arrive(1, k)
-
         combine(1, 0)
         combine(1, 1)
 
+    @pl.when(c == 0)
+    def _():
         @pl.loop(0, NK)
         def _(k):
-            @pl.when(c == 0)
-            def _():
-                forward(1, k).wait_recv()
-
-        rs = span(2)
-        for n in range(4):
-            cols = pl.ds(n * 256, 256)
-            acc[1, rs, cols] = sum(dot(chosen(2, k), w[k, :, cols]) for k in range(NK))
+            forward(1, k).wait_recv()
+
+    for n in range(4):
+        cols = pl.ds(n * 256, 256)
+        acc[1, span(2), cols] = sum(dot(chosen(2, k), w[k, :, cols]) for k in range(NK))
+    hidden(2)
 
     @pl.when(far == 0)
     def _():
-        @pl.loop(0, NK + 1)
-        def _(k):
-            @pl.when((c == 1) & (k < NK))
-            def _():
-                arrive(1, k)
-
-            @pl.when(k > 0)
-            def _():
-                gate_up(2, k - 1)
-
-            @pl.when(k >= NK - 1)
-            def _():
-                combine(1, k - NK + 1)
-
-    hidden(2)
+        combine(1, 0)
+        combine(1, 1)
+
     combine(1, 2)
     low_b = low_down(2)
 
@@ -556,39 +536,47 @@
     @pl.loop(0, NJ)
     def _(j):
         combine(2, j)
-
-    @pl.loop(0, NJ)
-    def _(j):
-        combine(0, j)
-        finish(j)
-
-    @pl.loop(0, NJ)
-    def _(j):
-        fin_send(j).wait_recv()
-        cols = pl.ds(pl.multiple_of((1 - c) * HALF + j * JC, JC), JC)
-        out[:, cols] = fin_got[j]
 
     meta_mirror.wait_send()
     meta_sibling.wait_send()
     meta_second.wait_send()
     wait_bytes(sel, s_x)
-    wait_bytes(back, s_ret)
     for part, fac in enumerate((fac_a, fac_b)):
         wait_bytes(fac.at[0, pl.ds(0, 3), 0], s_fac.at[part, 0])
         wait_bytes(fac.at[pl.ds(0, 3), :, 0], s_fac.at[part, 1])
         wait_bytes(fac.at[:, :, 0], s_fac.at[part, 2])
     for st in range(3):
         hid_send(st).wait_send()
-    for om in range(2):
-
-        @pl.loop(0, NK)
-        def _(k):
-            forward(om, k).wait_send()
+
+    @pl.loop(0, NK)
+    def _(k):
+        forward(0, k).wait_send()
+        forward(1, k).wait_send()
+        zrow(k).wait_send()
+        dw_send(k).wait_send()
+
+    def store_received(j):
+        fin_send(j).wait_recv()
+        cols = pl.ds(pl.multiple_of((1 - c) * HALF + j * JC, JC), JC)
+        out[:, cols] = fin_got[j]
 
     @pl.loop(0, NJ)
     def _(j):
-        zrow(j).wait_send()
-        dw_send(j).wait_send()
+        combine(0, j)
+        finish(j)
+
+        @pl.when(j >= 3)
+        def _():
+            store_received(j - 3)
+
+    @pl.loop(NJ - 3, NJ)
+    def _(j):
+        store_received(j)
+
+    wait_bytes(back, s_ret)
+
+    @pl.loop(0, NJ)
+    def _(j):
         zret(0, j).wait_send()
         zret(1, j).wait_send()
         fin_send(j).wait_send()

time: 67.3 us -> 66.4 us (0.987)
  Pallas kernels: 65.4 us -> 64.5 us
    pallas_call x1, Pallas kernels: 65.4 us -> 64.5 us  [on_device(): pl.pallas_call(kernel, out_shape=jax.ShapeDtypeStruct((ROWS, D), BF), in_...]
where the time goes in v4:
time: 66.4 us; the launch traced here: 66.3 us
  Pallas kernels  64.5 us (97%)
  local copies, waits for them, and re-layouts  1.82 us (3%)
    pallas_call x1, Pallas kernels, on_device(): pl.pallas_call(kernel, out_shape=jax.ShapeDtypeStruct((ROWS, D), BF), in_...  64.5 us
    unnamed x1, local copies, waits for them, and re-layouts  1.82 us

profile of v4, /device:TPU:1, one launch (start us, length us, event | category | flops | bytes accessed | tf_op | source)
XLA Modules:
  0.0 66.3 jit_solution(8921754788524918629)
XLA Ops:
  0.0 64.5 %expert_layer.1 = bf16[64,3584]{1,0:T(8,128)(2,1)} custom-call(bf16[64,3584]{1,0:T(8,128)(2,1)} %rows.1, s32[2,64]{1,0:T(2,128)} %bitcast.6, f32[2,64]{1,0:T(2,128)} %bitcast.7, bf16[1,3584,512]{2,1,0:T(8,128)(2,1)} %gate_w.1, bf16[1,3584,512]{2,1,0:T(8,128)(2,1)} %up_w.1, bf16[1,512,3584]{2,1,0:T(8,128)(2,1)} %down_w.1, bf16[8,64,224]{2,1,0:T(8,128)(2,1)} %bitcast.4, ...), custom_call_target="tpu_custom_call" | custom-call | flops 8589934592 | bytes 13631488 | tf_op jit(solution)/shard_map/expert_layer/pallas_call | solution.py:649
  64.5 1.8 %copy.14 = bf16[64,3584]{1,0:T(8,128)(2,1)} copy(bf16[64,3584]{1,0:T(8,128)(2,1)} %expert_layer.1) | data formatting | bytes 917504
